TPU v7x, 256 devices: a whole 4x4x8 slice. The times are simulated.
256 devices in a mesh: wide: 32 (over y, z), narrow: 8 (over x, core).
Axes of the slice: x: 4, y: 4, z: 8, core: 2. Of those that a mesh axis runs over, the one named last changes fastest.
Arguments:
- residual: bfloat16 [32, 8, 2048, 256], P('wide', 'narrow'), may hold values from -6 to 6
- scaling: float32 [32, 8, 2048], P('wide', 'narrow'), may hold values from 0.25 to 1
- local_inverse: bfloat16 [32, 8, 2048, 2048], P('wide', 'narrow'), may hold values from -0.125 to 0.125
- coarse_basis: bfloat16 [32, 8, 24, 2048], P('wide', 'narrow'), may hold values from -0.125 to 0.125
- primal_map: int32 [32, 8, 24], P('wide', 'narrow'), may hold values from 0 to 191
- slot_index: int32 [32, 8, 10, 256], P('wide', 'narrow'), may hold values from 0 to 2047, as said below
- slot_length: int32 [32, 8, 10], P('wide', 'narrow'), may hold values from 0 to 256, as said below
- coarse_sub: float32 [32, 192, 192], P('wide'), may hold values from -0.4375 to 0.4375
- coarse_pivot: float32 [32, 192, 192], P('wide'), as said below
Outputs:
- interface_sum: float32 [32, 8, 2048, 256], P('wide', 'narrow')
Inputs may be any that keep to these rules, and one draw needn't show every extreme that they name: `slot_index`: within one slot of one subdomain the 256 entries are distinct. `slot_length`: paired slots have equal lengths: slot j of subdomain (w, n) and slot n of (w, j); slot 8 of (w, n) and slot 9 of (w - 1, n). A subdomain's own narrow slot n, the slot 8 of slab 0 and the slot 9 of slab 32 - 1 have length 0. `coarse_pivot`: Symmetric.
All inputs are finite; a program needn't handle non-finite values.
Results may differ from a plain program's by a relative error of at most 0.0039.
The roundings to bfloat16 on the way count: a program that leaves them out, or rounds other values in their place, can miss the bound.
Values may be sent and summed in bfloat16 or wider, within the bound.
A program may use at most 128 MiB of HBM per device.

v0:
```python
import jax
import jax.numpy as jnp
from jax import lax
from jax.sharding import PartitionSpec as P

highest = lax.Precision.HIGHEST


def entering(part, axis, combine, identity, reverse):
    count = lax.axis_size(axis)
    place = lax.axis_index(axis)
    ahead = count - 1 - place if reverse else place
    gathered = jax.tree.map(lambda a: lax.all_gather(a, axis), part)
    state = jax.tree.map(lambda a, e: jnp.zeros_like(a) + jnp.asarray(e, a.dtype), part, identity)

    def one(turn, state):
        source = count - 1 - turn if reverse else turn
        return combine(
            state, jax.tree.map(lambda a: lax.dynamic_index_in_dim(a, source, 0, False), gathered)
        )

    return lax.fori_loop(0, ahead, one, state)


def shifted(block, axis, distance):
    devices = range(lax.axis_size(axis))
    route = [(i - distance, i) for i in devices if i - distance in devices]
    return lax.ppermute(block, axis, route)


def exact_dot(left, right):
    return jnp.dot(left, right, precision=highest, preferred_element_type=jnp.float32)


def compose(earlier, later):
    return (exact_dot(later[0], earlier[0]), exact_dot(later[0], earlier[1]) + later[1])


def coarse_solve(coarse_rhs, sub_block, pivot_block):
    order = sub_block.shape[0]
    identity = jnp.eye(order, dtype=jnp.float32)
    empty = jnp.zeros_like(coarse_rhs)
    sub_trans = sub_block.T
    before = entering((-sub_block, coarse_rhs), "wide", compose, (identity, empty), False)
    chain_y = coarse_rhs - exact_dot(sub_block, before[1])
    pivoted = exact_dot(pivot_block, chain_y)
    after = entering(
        (-sub_trans, exact_dot(sub_trans, pivoted)), "wide", compose, (identity, empty), True
    )
    return pivoted - after[1]


def body(
    residual,
    scaling,
    local_inverse,
    coarse_basis,
    primal_map,
    slot_index,
    slot_length,
    coarse_sub,
    coarse_pivot,
):
    groups = lax.axis_size("narrow")
    weights = scaling[0, 0]
    weighted = (weights[:, None] * residual[0, 0].astype(jnp.float32)).astype(jnp.bfloat16)
    local_part = jnp.dot(local_inverse[0, 0], weighted, preferred_element_type=jnp.float32)
    basis = coarse_basis[0, 0]
    primal = jnp.dot(basis, weighted, preferred_element_type=jnp.float32)
    order = coarse_sub.shape[1]
    one_hot = (primal_map[0, 0][:, None] == jnp.arange(order, dtype=jnp.int32)[None, :]).astype(
        jnp.float32
    )
    assembly = lax.dot_general(
        one_hot,
        primal,
        (((0,), (0,)), ((), ())),
        precision=highest,
        preferred_element_type=jnp.float32,
    )
    coarse_rhs = lax.psum(assembly, "narrow")
    coarse_sol = coarse_solve(coarse_rhs, coarse_sub[0], coarse_pivot[0])
    coarse_vals = exact_dot(one_hot, coarse_sol)
    spread = lax.dot_general(
        basis.astype(jnp.float32),
        coarse_vals,
        (((0,), (0,)), ((), ())),
        precision=highest,
        preferred_element_type=jnp.float32,
    )
    combined = (weights[:, None] * (local_part + spread)).astype(jnp.bfloat16)
    indices = slot_index[0, 0]
    lengths = slot_length[0, 0]
    capacity = indices.shape[1]
    live_mask = jnp.arange(capacity, dtype=jnp.int32)[None, :] < lengths[:, None]
    outgoing = jnp.where(live_mask[:, :, None], combined[indices], jnp.zeros((), jnp.bfloat16))
    narrow_in = lax.all_to_all(outgoing[:groups], "narrow", split_axis=0, concat_axis=0, tiled=True)
    below = shifted(outgoing[groups + 1], "wide", 1)
    above = shifted(outgoing[groups], "wide", -1)
    incoming = jnp.concatenate([narrow_in, below[None], above[None]], axis=0)
    columns = combined.shape[1]
    summed = (
        combined.astype(jnp.float32)
        .at[indices.reshape(-1)]
        .add(incoming.reshape(-1, columns).astype(jnp.float32))
    )
    return summed[None, None]


def solution(mesh):
    in_specs = (
        P("wide", "narrow", None, None),
        P("wide", "narrow", None),
        P("wide", "narrow", None, None),
        P("wide", "narrow", None, None),
        P("wide", "narrow", None),
        P("wide", "narrow", None, None),
        P("wide", "narrow", None),
        P("wide", None, None),
        P("wide", None, None),
    )
    out_specs = P("wide", "narrow", None, None)
    return jax.shard_map(body, mesh=mesh, in_specs=in_specs, out_specs=out_specs, check_vma=False)
```

profile of v0, /device:TPU:1, one launch (start us, length us, event | category | flops | bytes accessed | tf_op | source)
XLA Modules:
  0.0 475.1 jit_solution(10385188580187387895)
XLA Ops:
  7.4 2.1 fusion.15
  9.5 1.7 fusion.27
  11.2 0.0 all-gather.8.cloned.1.call-start
  11.3 0.7 neg.10
  12.0 0.0 all-gather.10.cloned.1.call-start
  12.0 66.6 %all-reduce.2.cloned.1.call-done = f32[192,256]{1,0:T(8,128)} async-done(((f32[192,256]{1,0:T(8,128)}), f32[192,256]{1,0:T(8,128)}) %all-reduce.2.cloned.1.call-update) | async-done | bytes 196624 | tf_op jit(solution)/shard_map/psum | solution.py:81
  78.7 0.1 copy.13
  78.8 0.7 fusion.23
  79.6 26.3 %all-gather.8.cloned.1.call-done = f32[32,192,192]{2,1,0:T(8,128)} async-done(((f32[1,192,192]{2,1,0:T(8,128)}), f32[32,192,192]{2,1,0:T(8,128)}) %all-gather.8.cloned.1.call-update) | async-done | bytes 4718608 | tf_op jit(solution)/shard_map/all_gather | solution.py:13
  105.9 88.2 %all-gather.10.cloned.1.call-done = f32[6144,256]{1,0:T(8,128)} async-done(((f32[192,256]{1,0:T(8,128)}), f32[6144,256]{1,0:T(8,128)}) %all-gather.10.cloned.1.call-update) | async-done | bytes 6291472 | tf_op jit(solution)/shard_map/all_gather | solution.py:13
  194.3 0.9 copy-done.2
  195.1 0.3 fusion.13
  195.5 0.3 fusion.21
  195.8 1.3 convolution_bitcast_fusion
  197.2 0.1 iota_compare_fusion.2
  197.3 6.5 %fusion.6 = f32[256,2048]{1,0:T(8,128)S(1)} fusion(bf16[1,1,2048,2048]{3,2,1,0:T(8,128)(2,1)} %param.15, bf16[1,1,2048,256]{3,2,1,0:T(8,128)(2,1)} %param.13, f32[2048]{0:T(1024)S(1)} %bitcast.96), kind=kOutput, calls=%fused_computation.10 | convolution fusion | flops 2149056512 | bytes 11542528 | tf_op jit(solution)/shard_map/dot_general | solution.py:67
  203.7 78.7 %all-gather.12.cloned.1.call-done = f32[6144,192]{1,0:T(8,128)} async-done(((f32[192,192]{1,0:T(8,128)}), f32[6144,192]{1,0:T(8,128)}) %all-gather.12.cloned.1.call-update) | async-done | bytes 4718608 | tf_op jit(solution)/shard_map/all_gather | solution.py:13
  282.5 88.4 %all-gather.14.cloned.1.call-done = f32[6144,256]{1,0:T(8,128)} async-done(((f32[192,256]{1,0:T(8,128)}), f32[6144,256]{1,0:T(8,128)}) %all-gather.14.cloned.1.call-update) | async-done | bytes 6291472 | tf_op jit(solution)/shard_map/all_gather | solution.py:13
  370.9 43.4 %while.27 = (s32[]{:T(128)}, f32[192,256]{1,0:T(8,128)S(1)}, s32[]{:T(128)}, f32[32,192,192]{2,1,0:T(8,128)}, f32[32,192,256]{2,1,0:T(8,128)}, /*index=5*/s32[]{:T(128)}, s32[]{:T(128)}, s32[]{:T(128)}, s32[]{:T(128)}) while((s32[]{:T(128)}, f32[192,256]{1,0:T(8,128)S(1)}, s32[]{:T(128)}, f32[32,192,192]{2,1,0:T(8,128)}, ...), condition=%wide.region_4.5_spmd, body=%wide.region_3.4_spmd.sunk | while | flops 113295368 | bytes 1180811 | solution.py:22
  371.0 1.3 convolution_add_fusion.6
  372.4 1.3 convolution_add_fusion.6
  373.8 1.3 convolution_add_fusion.6
  375.2 1.3 convolution_add_fusion.6
  376.6 1.3 convolution_add_fusion.6
  378.0 1.3 convolution_add_fusion.6
  379.4 1.3 convolution_add_fusion.6
  380.8 1.3 convolution_add_fusion.6
  382.2 1.3 convolution_add_fusion.6
  383.6 1.3 convolution_add_fusion.6
  385.0 1.3 convolution_add_fusion.6
  386.4 1.3 convolution_add_fusion.6
  387.8 1.3 convolution_add_fusion.6
  389.2 1.3 convolution_add_fusion.6
  390.6 1.3 convolution_add_fusion.6
  392.0 1.3 convolution_add_fusion.6
  393.4 1.3 convolution_add_fusion.6
  394.8 1.3 convolution_add_fusion.6
  396.2 1.3 convolution_add_fusion.6
  397.6 1.3 convolution_add_fusion.6
  399.0 1.3 convolution_add_fusion.6
  400.4 1.3 convolution_add_fusion.6
  401.8 1.3 convolution_add_fusion.6
  403.2 1.3 convolution_add_fusion.6
  404.6 1.3 convolution_add_fusion.6
  406.0 1.3 convolution_add_fusion.6
  407.4 1.3 convolution_add_fusion.6
  408.8 1.3 convolution_add_fusion.6
  410.2 1.3 convolution_add_fusion.6
  411.6 1.3 convolution_add_fusion.6
  413.0 1.3 convolution_add_fusion.6
  414.4 0.2 fusion.20
  414.6 2.0 fusion.12
  416.6 0.5 copy.14
  417.1 8.1 %gather_fusion = bf16[2560,256]{1,0:T(8,128)(2,1)} fusion(bf16[2048,256]{1,0:T(8,128)(2,1)S(1)} %copy.14, s32[3072]{0:T(1024)S(1)} %pad_clamp_fusion), kind=kCustom, calls=%fused_computation | custom fusion | bytes 2631680 | tf_op jit(solution)/shard_map/gather | solution.py:96
  425.3 1.6 broadcast_select_fusion
  426.9 1.1 slice.14
  428.0 5.6 %all-to-all-start = ((bf16[8,256,256]{2,1,0:T(8,128)(2,1)}), bf16[8,256,256]{2,1,0:T(8,128)(2,1)}, u32[]{:S(2)}, u32[]{:S(2)}) async-start(bf16[8,256,256]{2,1,0:T(8,128)(2,1)} %slice.14), calls=%async_computation | async-start | bytes 2097152 | tf_op jit(solution)/shard_map/all_to_all | solution.py:97
  433.7 1.7 collective-permute-start
  435.4 1.3 collective-permute-start.1
  436.8 1.6 copy.15
  438.4 3.8 collective-permute-done.1
  442.2 6.7 %all-to-all-done = bf16[8,256,256]{2,1,0:T(8,128)(2,1)} async-done(((bf16[8,256,256]{2,1,0:T(8,128)(2,1)}), bf16[8,256,256]{2,1,0:T(8,128)(2,1)}, u32[]{:S(2)}, u32[]{:S(2)}) %all-to-all-start) | async-done | bytes 1048608 | tf_op jit(solution)/shard_map/all_to_all | solution.py:97
  448.8 1.4 pad_maximum_fusion
  450.2 17.2 %scatter_custom_fusion = f32[2048,256]{1,0:T(8,128)} fusion(f32[2048,256]{1,0:T(8,128)} %copy.15, s32[2560]{0:T(1024)S(1)} %fusion.32, bf16[2560,256]{1,0:T(8,128)(2,1)S(1)} %bitcast.86), kind=kCustom, calls=%fused_computation.14 | custom fusion | flops 1310720 | bytes 3407872 | tf_op jit(solution)/shard_map/scatter-add | solution.py:105
  (63 shorter events, 0.8 us)
Async XLA Ops:
  7.4 188.1 %copy-start = (f32[1,192,192]{2,1,0:T(8,128)S(1)}, f32[1,192,192]{2,1,0:T(8,128)}, u32[]{:S(2)}) copy-start(f32[1,192,192]{2,1,0:T(8,128)} %param.21) | copy-start | bytes 442372
  7.4 3.9 copy-start.1
  7.4 71.3 %all-reduce.2.cloned.1.call-start = ((), (), s32[]{:S(2)}) async-start(), calls=%async_computation.1 | async-start | bytes 393216 | tf_op jit(solution)/shard_map/psum | solution.py:81
  11.2 94.7 %all-gather.8.cloned.1.call-start = ((), (), s32[]{:S(2)}) async-start(), calls=%async_computation.2 | async-start | bytes 6488064 | tf_op jit(solution)/shard_map/all_gather | solution.py:13
  12.0 182.2 %all-gather.10.cloned.1.call-start = ((), (), s32[]{:S(2)}) async-start(), calls=%async_computation.3 | async-start | bytes 6488064 | tf_op jit(solution)/shard_map/all_gather | solution.py:13
  78.7 203.8 %all-gather.12.cloned.1.call-start = ((), (), s32[]{:S(2)}) async-start(), calls=%async_computation.4 | async-start | bytes 6488064 | tf_op jit(solution)/shard_map/all_gather | solution.py:13
  79.6 291.3 %all-gather.14.cloned.1.call-start = ((), (), s32[]{:S(2)}) async-start(), calls=%async_computation.5 | async-start | bytes 6488064 | tf_op jit(solution)/shard_map/all_gather | solution.py:13
  194.2 0.9 copy-start.2
  194.2 2.9 copy-start.3
  194.2 2.9 copy-start.7
  194.2 3.0 copy-start.5
  370.9 43.4 %copy-start.6 = (s32[1,1,24]{2,1,0:T(1,128)S(1)}, s32[1,1,24]{2,1,0:T(1,128)}, u32[]{:S(2)}) copy-start(s32[1,1,24]{2,1,0:T(1,128)} %param.17) | copy-start | bytes 292
  426.9 9.8 %copy-start.4 = (s32[1,1,10,256]{3,1,2,0:T(1,128)S(1)}, s32[1,1,10,256]{3,1,2,0:T(1,128)}, u32[]{:S(2)}) copy-start(s32[1,1,10,256]{3,1,2,0:T(1,128)} %param.18) | copy-start | bytes 30724
  428.0 20.8 %all-to-all-start = ((bf16[8,256,256]{2,1,0:T(8,128)(2,1)}), bf16[8,256,256]{2,1,0:T(8,128)(2,1)}, u32[]{:S(2)}, u32[]{:S(2)}) async-start(bf16[8,256,256]{2,1,0:T(8,128)(2,1)} %slice.14), calls=%async_computation | async-start | bytes 2097152 | tf_op jit(solution)/shard_map/all_to_all | solution.py:97
  433.7 4.7 collective-permute-start
  435.4 6.8 %collective-permute-start.1 = (bf16[256,256]{1,0:T(8,128)(2,1)S(1)}, bf16[256,256]{1,0:T(8,128)(2,1)S(1)}, u32[]{:S(2)}, u32[]{:S(2)}) collective-permute-start(bf16[256,256]{1,0:T(8,128)(2,1)S(1)} %get-tuple-element.156), channel_id=1, source_target_pairs={{8,0},{16,8},{24,16},{32,24},{40,32},{48,40},{56,48},{64,56},{72,6... | collective-permute-start | bytes 393224 | tf_op jit(solution)/shard_map/ppermute | solution.py:28
Sparse Core Ops, SparseCore 0:
  11.3 67.2 all-reduce.1
Sparse Core Ops, SparseCore 1:
  14.3 91.6 all-gather.7
  108.7 85.4 all-gather.9
  197.0 85.5 all-gather.11
  285.4 85.4 all-gather.13
where the time goes:
time: 476 us; the launch traced here: 475 us
  waiting for transfers between devices  359 us (75%)
  matrix products  56.1 us (12%)
  other arithmetic  21.8 us (5%)
  between operations  15.3 us (3%)
  local copies, waits for them, and re-layouts  12.9 us (3%)
  starting transfers between devices  8.84 us (2%)
    all_gather x4, waiting for transfers between devices, entering(): gathered = jax.tree.map(lambda a: lax.all_gather(a, axis), part)  282 us
    psum x1, waiting for transfers between devices, body(): coarse_rhs = lax.psum(assembly, 'narrow')  66.6 us
    dot_general x35, matrix products, exact_dot(): jnp.dot(left, right, precision=highest, preferred_element_type=jnp.float32)  43.8 us
    scatter-add x1, other arithmetic, body(): summed = combined.astype(jnp.float32).at[indices.reshape(-1)].add(incomin...  17.2 us
  transfers between devices with their start and end apart: 8, of which 7 were waited for; matrix products, arithmetic and copies ran while one was open for 2% of the time, Pallas kernels for 0%

commit v1 on v0

v1 whole, which is shorter than its diff:
```python
import jax
import jax.numpy as jnp
from jax import lax
from jax.experimental import pallas as pl
from jax.experimental.pallas import tpu as pltpu
from jax.sharding import PartitionSpec as P

MESH = pl.DeviceIdType.MESH
f32 = jnp.float32
bf16 = jnp.bfloat16
NZ = 8
NY = 4
NN = 8
NS = 10
NI = 2048
R = 256
PC = 24
G = 192
CH = R // NN
PIECE = G // NN
CARRY = CH + G
TILE = 256


def owner_z(n):
    return n // 2 + 4 * (n % 2)


def iota(shape, axis):
    return lax.broadcasted_iota(jnp.int32, shape, axis)


def split2(a):
    high = a.astype(bf16)
    return high, (a - high.astype(f32)).astype(bf16)


def split3(a):
    high = a.astype(bf16)
    rest = a - high.astype(f32)
    middle = rest.astype(bf16)
    return high, middle, (rest - middle.astype(f32)).astype(bf16)


def nn(a, b):
    return lax.dot_general(a, b, (((1,), (0,)), ((), ())), preferred_element_type=f32)


def nt(a, b):
    return lax.dot_general(a, b, (((1,), (1,)), ((), ())), preferred_element_type=f32)


def dot3(dot, a, b):
    a_high, a_low = split2(a)
    b_high, b_low = split2(b)
    return dot(a_high, b_high) + (dot(a_high, b_low) + dot(a_low, b_high))


def kernel(
    res_hbm, scal_ref, inv_hbm, basis_ref, pmap_ref, sidx_ref, slen_ref, sub_hbm, piv_hbm,
    out_hbm,
    res, inv, wgt, local, rows, ext, select, pick_out, pick_in, inc, result,
    idxm, tiles, maps, spread_map, vals, xfull, stack,
    prim_in, prim_v, sub, piv, chain, rhs, planes, high_carry, pivoted, xs, xplanes, carry,
    load_sem, inv_sem, out_sem,
    prim_send, prim_recv, sub_send, sub_recv, piv_send, piv_recv,
    map_send, map_recv, pick_send, pick_recv,
    y_send, y_recv, t_send, t_recv, b_send, b_recv,
    x_send, x_recv, gather_send, gather_recv, val_send, val_recv,
):
    w = lax.axis_index("wide")
    n = lax.axis_index("narrow")
    y = w // NZ
    z = w % NZ
    base = y * NZ
    above = lax.rem(w + 1, NY * NZ)
    below = lax.rem(w + NY * NZ - 1, NY * NZ)
    is_owner = z == owner_z(n)

    load = pltpu.make_async_copy(res_hbm.at[0, 0], res, load_sem)
    load.start()

    def inv_load(i):
        at = pl.ds(pl.multiple_of(i * TILE, TILE), TILE)
        return pltpu.make_async_copy(inv_hbm.at[0, 0, at], inv.at[at], inv_sem.at[i])

    @pl.loop(0, NI // TILE)
    def _(i):
        inv_load(i).start()

    barrier = pltpu.get_barrier_semaphore()

    def hello(device):
        pl.semaphore_signal(barrier, inc=1, device_id=device, device_id_type=MESH)

    for d in range(1, NN):
        hello((w, lax.rem(n + d, NN)))
    hello((above, n))
    hello((below, n))

    @pl.when(is_owner)
    def _():
        @pl.loop(1, NZ * NN)
        def _(d):
            at = lax.rem(z * NN + n + d, NZ * NN)
            hello((base + at // NN, at % NN))

        for d in range(1, NY):
            hello((lax.rem(y + d, NY) * NZ + z, n))

    @pl.when(jnp.logical_not(is_owner))
    def _():
        hello((base + owner_z(n), n))

    basis = basis_ref[0, 0]
    scal = scal_ref[0]
    stack[...] = jnp.zeros_like(stack)
    for c in range(3):
        stack[32 * c : 32 * c + PC] = basis.astype(f32)
    for c, term in enumerate(split3(scal)):
        stack[96 + c : 97 + c] = term.astype(f32)
    stack[99:100] = scal
    for i in range(NI // 128):
        ext[128 * i : 128 * i + 128] = stack[:, 128 * i : 128 * i + 128].T
    load.wait()
    wgt[...] = (ext[:, 99:100] * res[...].astype(f32)).astype(bf16)
    primal = nn(basis, wgt[...])

    pm = jnp.broadcast_to(pmap_ref[0].astype(f32), (PC, PC))
    map_col = jnp.sum(jnp.where(iota((PC, PC), 0) == iota((PC, PC), 1), pm, 0.0), axis=1, keepdims=True)
    lane = iota((8, 128), 1)
    map_tile = jnp.zeros((8, 128), f32)
    for a in range(3):
        map_tile = jnp.where(lane == 96 + a, map_col[8 * a : 8 * a + 8], map_tile)
    for half in range(2):
        for m in range(4):
            tile = map_tile
            for a in range(3):
                piece = primal[8 * a : 8 * a + 8, 128 * half : 128 * half + 128]
                shift = 32 * ((a - m) % 4)
                if shift:
                    piece = pltpu.roll(piece, shift, 1)
                tile = jnp.where(lane // 32 == a, piece, tile)
            tiles[4 * half + m] = tile

    pl.semaphore_wait(barrier, (NN - 1) + 2 + NN + 9 * is_owner.astype(jnp.int32))

    def owned(c):
        return jnp.logical_and(is_owner, c == n)

    def deliver(src, dst, send, recv, device, here):
        @pl.when(here)
        def _():
            pltpu.make_async_copy(src, dst, recv).start()

        @pl.when(jnp.logical_not(here))
        def _():
            pltpu.make_async_remote_copy(
                src_ref=src, dst_ref=dst, send_sem=send, recv_sem=recv, device_id=device, device_id_type=MESH
            ).start()

    def sent(src, dst, send, recv, device, here):
        @pl.when(jnp.logical_not(here))
        def _():
            pltpu.make_async_remote_copy(
                src_ref=src, dst_ref=dst, send_sem=send, recv_sem=recv, device_id=device, device_id_type=MESH
            ).wait_send()

    piece_at = pl.ds(pl.multiple_of(n * PIECE, 8), PIECE)

    def prim_args(c):
        return (tiles.at[c], prim_in.at[z * NN + n], prim_send.at[c], prim_recv, (base + owner_z(c), c), owned(c))

    def sub_args(c):
        return (sub_hbm.at[0, piece_at], sub.at[z, piece_at], sub_send.at[c], sub_recv.at[z], (base + owner_z(c), c), owned(c))

    def piv_args(c):
        return (piv_hbm.at[0, piece_at], piv.at[z, piece_at], piv_send.at[c], piv_recv, (base + owner_z(c), c), owned(c))

    def map_copy(c):
        return pltpu.make_async_remote_copy(
            src_ref=tiles.at[0], dst_ref=maps.at[n], send_sem=map_send.at[c], recv_sem=map_recv.at[n],
            device_id=(w, c), device_id_type=MESH,
        )

    def in_map(c):
        return pltpu.make_async_copy(maps.at[c], maps.at[c], map_recv.at[c])

    for args in (prim_args, sub_args):
        @pl.loop(0, NN)
        def _(c, args=args):
            deliver(*args(c))

    @pl.loop(0, NN)
    def _(c):
        deliver(*piv_args(c))

        @pl.when(c != n)
        def _():
            map_copy(c).start()

    maps[n] = tiles[0]

    rows[:, 512:640] = ext[...].astype(bf16)

    @pl.loop(0, NI // TILE)
    def _(i):
        at = pl.ds(pl.multiple_of(i * TILE, TILE), TILE)
        inv_load(i).wait()
        part = nn(inv[at], wgt[...])
        local[at] = part
        high, low = split2(part)
        rows[at, 0:256] = high
        rows[at, 256:512] = low

    slot_lane = iota((1, TILE), 1)
    for k in range(NS):
        idxm[k : k + 1] = jnp.where(slot_lane < slen_ref[0, 0, k], sidx_ref[0, 0, k : k + 1], -1)

    def pick_copy(k):
        to_w = jnp.where(k == 8, below, jnp.where(k == 9, above, w))
        to_n = jnp.where(k < 8, k, n)
        slot = jnp.where(k == 8, 9, jnp.where(k == 9, 8, n))
        return pltpu.make_async_remote_copy(
            src_ref=pick_out.at[k], dst_ref=pick_in.at[slot], send_sem=pick_send.at[k], recv_sem=pick_recv.at[slot],
            device_id=(to_w, to_n), device_id_type=MESH,
        )

    def in_pick(k):
        return pltpu.make_async_copy(pick_in.at[k], pick_in.at[k], pick_recv.at[k])

    @pl.loop(0, NS)
    def _(k):
        @pl.when(k != n)
        def _():
            row = jnp.broadcast_to(idxm[pl.ds(k, 1)].astype(f32), (TILE, TILE))
            col = jnp.sum(jnp.where(iota((TILE, TILE), 0) == iota((TILE, TILE), 1), row, 0.0), axis=1, keepdims=True)
            hot = jnp.where(col.astype(jnp.int32) == iota((TILE, NI), 1), 1.0, 0.0).astype(bf16)
            pick_out[k] = nn(hot, rows[...]).astype(bf16)
            pick_copy(k).start()

    def y_copies(d):
        device = (lax.rem(y + d, NY) * NZ + z, n)
        return [
            pltpu.make_async_remote_copy(
                src_ref=chain.at[NZ - 1, part], dst_ref=planes.at[y, part], send_sem=send.at[d - 1], recv_sem=recv.at[y],
                device_id=device, device_id_type=MESH,
            )
            for part, send, recv in ((pl.ds(0, CH), y_send, y_recv), (pl.ds(CH, G), t_send, t_recv))
        ]

    def back_copy(d):
        return pltpu.make_async_remote_copy(
            src_ref=xplanes.at[y], dst_ref=xplanes.at[y], send_sem=b_send.at[d - 1], recv_sem=b_recv.at[y],
            device_id=(lax.rem(y + d, NY) * NZ + z, n), device_id_type=MESH,
        )

    chunk_at = pl.ds(pl.multiple_of(n * CH, CH), CH)

    def x_args(v):
        return (xs.at[v], xfull.at[chunk_at], x_send.at[v], x_recv, (base + v, n), v == z)

    @pl.when(is_owner)
    def _():
        pltpu.make_async_copy(prim_in, prim_in, prim_recv).wait()

        @pl.loop(0, NZ)
        def _(v):
            hots = []
            for c in range(NN):
                tile = prim_in[v * NN + c]
                for a in range(3):
                    at = PC * c + 8 * a
                    prim_v[at : at + 8] = pltpu.roll(tile, 128 - 32 * a, 1) if a else tile
                    col = tile[:, 96 + a : 97 + a].astype(jnp.int32)
                    hots.append(jnp.where(col == iota((8, G), 1), 1.0, 0.0))
            hot = jnp.concatenate(hots, axis=0).astype(bf16)
            high, middle, low = split3(prim_v[...].T[:CH])
            rhs[v] = nn(high, hot) + (nn(middle, hot) + nn(low, hot))

        def in_sub(v):
            pltpu.make_async_copy(sub.at[v], sub.at[v], sub_recv.at[v]).wait()

        eye = jnp.where(iota((G, G), 0) == iota((G, G), 1), 1.0, 0.0)
        in_sub(0)
        chain[0, 0:CH] = rhs[0]
        first_high, first_low = split2(sub[0])
        chain[0, CH:CARRY] = -(nt(eye.astype(bf16), first_high) + nt(eye.astype(bf16), first_low))

        @pl.loop(1, NZ)
        def _(v):
            in_sub(v)
            step = dot3(nt, chain[v - 1], sub[v])
            chain[v, 0:CH] = rhs[v] - step[0:CH]
            chain[v, CH:CARRY] = -step[CH:CARRY]

        for d in range(1, NY):
            y_copies(d)[0].start()
        for d in range(1, NY):
            y_copies(d)[1].start()
        planes[y] = chain[NZ - 1]
        high_carry[NZ - 1] = -eye

        @pl.loop(0, NZ - 1)
        def _(i):
            v = NZ - 2 - i
            high_carry[v] = -dot3(nn, high_carry[v + 1], sub[v + 1])

        pltpu.make_async_copy(piv, piv, piv_recv).wait()

    @pl.loop(0, NI // TILE)
    def _(i):
        at = pl.ds(pl.multiple_of(i * TILE, TILE), TILE)
        row_id = iota((TILE, TILE), 0) + i * TILE
        for k in range(NS):
            select[at, TILE * k : TILE * k + TILE] = jnp.where(idxm[k : k + 1] == row_id, 1.0, 0.0).astype(bf16)

    @pl.loop(0, NN)
    def _(c):
        @pl.when(c != n)
        def _():
            in_map(c).wait()

    for c in range(NN):
        tile = maps[c]
        for a in range(3):
            col = tile[:, 96 + a : 97 + a].astype(jnp.int32)
            spread_map[32 * c + 8 * a : 32 * c + 8 * a + 8] = jnp.where(col == iota((8, G), 1), 1.0, 0.0)
        spread_map[32 * c + PC : 32 * c + 32] = jnp.zeros((32 - PC, G), f32)
    vals[:, 96:128] = jnp.zeros((NS, 32, R), bf16)

    @pl.when(is_owner)
    def _():
        def in_plane(d):
            src = lax.rem(y + NY - d, NY)
            for part, recv in ((pl.ds(0, CH), y_recv), (pl.ds(CH, G), t_recv)):
                pltpu.make_async_copy(planes.at[src, part], planes.at[src, part], recv.at[src]).wait()

        for d in range(1, NY):
            in_plane(d)
        carry[...] = jnp.where(y > 0, planes[0, 0:CH], 0.0)
        for g in range(1, NY - 1):
            @pl.when(y > g)
            def _(g=g):
                carry[...] = planes[g, 0:CH] + dot3(nn, carry[...], planes[g, CH:CARRY])

        for v in range(NZ):
            solved = chain[v, 0:CH] + dot3(nn, carry[...], chain[v, CH:CARRY])
            pivoted[v] = dot3(nn, solved, piv[v])
        xs[NZ - 1] = pivoted[NZ - 1]

        @pl.loop(0, NZ - 1)
        def _(i):
            v = NZ - 2 - i
            xs[v] = pivoted[v] - dot3(nn, xs[v + 1], sub[v + 1])

        xplanes[y] = dot3(nn, xs[0], sub[0])
        for d in range(1, NY):
            back_copy(d).start()
        for d in range(1, NY):
            src = lax.rem(y + NY - d, NY)
            pltpu.make_async_copy(xplanes.at[src], xplanes.at[src], b_recv.at[src]).wait()
        carry[...] = jnp.where(y < NY - 1, xplanes[NY - 1], 0.0)
        for g in range(NY - 2, 0, -1):
            @pl.when(y < g)
            def _(g=g):
                carry[...] = xplanes[g] + dot3(nt, carry[...], planes[g, CH:CARRY])

        for v in range(NZ):
            xs[v] = xs[v] + dot3(nn, carry[...], high_carry[v])

        @pl.loop(0, NZ)
        def _(v):
            deliver(*x_args(v))

    def gather_copy(c):
        return pltpu.make_async_remote_copy(
            src_ref=xfull.at[chunk_at], dst_ref=xfull.at[chunk_at], send_sem=gather_send.at[c], recv_sem=gather_recv.at[n],
            device_id=(w, c), device_id_type=MESH,
        )

    pltpu.make_async_copy(xfull.at[chunk_at], xfull.at[chunk_at], x_recv).wait()

    @pl.loop(1, NN)
    def _(d):
        gather_copy(lax.rem(n + d, NN)).start()

    @pl.loop(1, NN)
    def _(d):
        src = lax.rem(n + d, NN)
        at = pl.ds(pl.multiple_of(src * CH, CH), CH)
        pltpu.make_async_copy(xfull.at[at], xfull.at[at], gather_recv.at[src]).wait()

    hot = spread_map[...].astype(bf16)
    for c, term in enumerate(split3(xfull[...])):
        picked = nt(hot, term).astype(bf16)
        for j in range(NN):
            vals[j, 32 * c : 32 * c + 32] = picked[32 * j : 32 * j + 32]

    def val_copy(side):
        return pltpu.make_async_remote_copy(
            src_ref=vals.at[n, pl.ds(0, 96)], dst_ref=vals.at[8 + side, pl.ds(0, 96)],
            send_sem=val_send.at[side], recv_sem=val_recv.at[side],
            device_id=(above if side == 0 else below, n), device_id_type=MESH,
        )

    for side in range(2):
        val_copy(side).start()

    def receive(k):
        in_pick(k).wait()
        picked = pick_in[k]
        spread = nn(picked[:, 512:640], vals[k])
        weight = jnp.sum(picked[:, 608:611].astype(f32), axis=1, keepdims=True)
        part = picked[:, 0:256].astype(f32) + picked[:, 256:512].astype(f32)
        at = pl.ds(pl.multiple_of(k * TILE, TILE), TILE)
        inc[at] = (weight * (part + spread)).astype(bf16)

    @pl.loop(0, NN)
    def _(k):
        @pl.when(k != n)
        def _():
            receive(k)

    own_at = pl.ds(pl.multiple_of(n * TILE, TILE), TILE)
    inc[own_at] = jnp.zeros((TILE, R), bf16)

    @pl.loop(0, NI // TILE)
    def _(i):
        at = pl.ds(pl.multiple_of(i * TILE, TILE), TILE)
        spread = nn(rows[at, 512:640], vals[n])
        combined = (ext[at, 99:100] * (local[at] + spread)).astype(bf16)
        result[at] = combined.astype(f32)

    for side in range(2):
        into = vals.at[8 + side, pl.ds(0, 96)]
        pltpu.make_async_copy(into, into, val_recv.at[side]).wait()
        receive(8 + side)

    def store(i):
        at = pl.ds(pl.multiple_of(i * TILE, TILE), TILE)
        return pltpu.make_async_copy(result.at[at], out_hbm.at[0, 0, at], out_sem.at[i])

    @pl.loop(0, NI // TILE)
    def _(i):
        at = pl.ds(pl.multiple_of(i * TILE, TILE), TILE)
        result[at] += nn(select[at], inc[...])
        store(i).start()

    @pl.loop(0, NN)
    def _(c):
        sent(*prim_args(c))
        sent(*sub_args(c))
        sent(*piv_args(c))

        @pl.when(c != n)
        def _():
            map_copy(c).wait_send()
            gather_copy(c).wait_send()

    @pl.loop(0, NS)
    def _(k):
        @pl.when(k != n)
        def _():
            pick_copy(k).wait_send()

    for side in range(2):
        val_copy(side).wait_send()

    @pl.when(is_owner)
    def _():
        for d in range(1, NY):
            for copy in y_copies(d):
                copy.wait_send()
            back_copy(d).wait_send()

        @pl.loop(0, NZ)
        def _(v):
            sent(*x_args(v))

    @pl.loop(0, NI // TILE)
    def _(i):
        store(i).wait()


def body(residual, scaling, inverse, basis, primal_map, slot_index, slot_length, sub, pivot):
    vmem = pl.BlockSpec(memory_space=pltpu.VMEM)
    smem = pl.BlockSpec(memory_space=pltpu.SMEM)
    hbm = pl.BlockSpec(memory_space=pl.ANY)
    dma = pltpu.SemaphoreType.DMA
    V = pltpu.VMEM
    return pl.pallas_call(
        kernel,
        out_shape=jax.ShapeDtypeStruct((1, 1, NI, R), f32),
        in_specs=[hbm, vmem, hbm, vmem, vmem, vmem, smem, hbm, hbm],
        out_specs=hbm,
        scratch_shapes=[
            V((NI, R), bf16), V((NI, NI), bf16), V((NI, R), bf16), V((NI, R), f32), V((NI, 640), bf16), V((NI, 128), f32),
            V((NI, NS * TILE), bf16), V((NS, TILE, 640), bf16), V((NS, TILE, 640), bf16), V((NS * TILE, R), bf16), V((NI, R), f32),
            V((16, TILE), jnp.int32), V((NN, 8, 128), f32), V((NN, 8, 128), f32), V((NN * 32, G), f32), V((NS, 128, R), bf16),
            V((R, G), f32), V((128, NI), f32),
            V((NZ * NN, 8, 128), f32), V((G, 128), f32), V((NZ, G, G), f32), V((NZ, G, G), f32), V((NZ, CARRY, G), f32),
            V((NZ, CH, G), f32), V((NY, CARRY, G), f32), V((NZ, G, G), f32), V((NZ, CH, G), f32), V((NZ, CH, G), f32),
            V((NY, CH, G), f32), V((CH, G), f32),
            dma, dma((NI // TILE,)), dma((NI // TILE,)),
            dma((NN,)), dma, dma((NN,)), dma((NZ,)), dma((NN,)), dma,
            dma((NN,)), dma((NN,)), dma((NS,)), dma((NS,)),
            dma((NY - 1,)), dma((NY,)), dma((NY - 1,)), dma((NY,)), dma((NY - 1,)), dma((NY,)),
            dma((NZ,)), dma, dma((NN,)), dma((NN,)), dma((2,)), dma((2,)),
        ],
        compiler_params=pltpu.CompilerParams(collective_id=0, has_side_effects=True, vmem_limit_bytes=58 * 2**20),
    )(residual, scaling, inverse, basis, primal_map, slot_index, slot_length, sub, pivot)


def solution(mesh):
    in_specs = (
        P("wide", "narrow", None, None),
        P("wide", "narrow", None),
        P("wide", "narrow", None, None),
        P("wide", "narrow", None, None),
        P("wide", "narrow", None),
        P("wide", "narrow", None, None),
        P("wide", "narrow", None),
        P("wide", None, None),
        P("wide", None, None),
    )
    out_specs = P("wide", "narrow", None, None)
    return jax.shard_map(body, mesh=mesh, in_specs=in_specs, out_specs=out_specs, check_vma=False)
```

time: 476 us -> 87.3 us (0.18)
  waiting for transfers between devices: 359 us -> 0 us
  Pallas kernels: 0 us -> 82.7 us
  matrix products: 56.1 us -> 0 us
  other arithmetic: 21.8 us -> 0 us
  between operations: 15.3 us -> 0.01 us
  starting transfers between devices: 8.84 us -> 0 us
  local copies, waits for them, and re-layouts: 12.9 us -> 4.35 us
    all_gather x4 -> x0, waiting for transfers between devices: 282 us -> none  [entering(): gathered = jax.tree.map(lambda a: lax.all_gather(a, axis), part)]
    pallas_call x0 -> x1, Pallas kernels: none -> 82.7 us  [body(): pl.pallas_call(kernel, out_shape=jax.ShapeDtypeStruct((1, 1, NI, R), f32)...]
    psum x1 -> x0, waiting for transfers between devices: 66.6 us -> none  [body(): coarse_rhs = lax.psum(assembly, 'narrow')]
    dot_general x39 -> x0, matrix products: 56.1 us -> none  [the longest x35 43.8 us: exact_dot(): jnp.dot(left, right, precision=highest, preferred_element_type=jnp.float32)]
    scatter-add x1 -> x0, other arithmetic: 17.2 us -> none  [body(): summed = combined.astype(jnp.float32).at[indices.reshape(-1)].add(incomin...]
    gather x1 -> x0, local copies, waits for them, and re-layouts: 8.15 us -> none  [body(): combined[indices]]
    all_to_all x1 -> x0, waiting for transfers between devices: 6.67 us -> none  [body(): lax.all_to_all(outgoing[:groups], 'narrow', split_axis=0, concat_axis=0,...]
    all_to_all x1 -> x0, starting transfers between devices: 5.64 us -> none  [body(): lax.all_to_all(outgoing[:groups], 'narrow', split_axis=0, concat_axis=0,...]
  transfers between devices with their start and end apart: 8 -> 0, of which waited for: 7 -> 0; matrix products, arithmetic and copies ran while one was open for 2% -> 0% of each run, Pallas kernels for 0% -> 0%
where the time goes in v1:
time: 87.3 us; the launch traced here: 87.1 us
  Pallas kernels  82.7 us (95%)
  local copies, waits for them, and re-layouts  4.35 us (5%)
    pallas_call x1, Pallas kernels, body(): pl.pallas_call(kernel, out_shape=jax.ShapeDtypeStruct((1, 1, NI, R), f32)...  82.7 us
    unnamed x2, local copies, waits for them, and re-layouts  4.35 us

profile of v1, /device:TPU:1, one launch (start us, length us, event | category | flops | bytes accessed | tf_op | source)
XLA Modules:
  0.0 87.1 jit_solution(14734683364446313762)
XLA Ops:
  0.0 1.3 %copy.10.sidx_ref = s32[1,1,10,256]{3,2,1,0:T(8,128)} copy(s32[1,1,10,256]{3,1,2,0:T(1,128)} %param.14) | data formatting | bytes 20480 | tf_op args[5]
  1.3 82.7 %shard_map.91 = f32[1,1,2048,256]{3,2,1,0:T(8,128)} custom-call(bf16[1,1,2048,256]{3,2,1,0:T(8,128)(2,1)} %res_hbm.1, f32[1,1,2048]{2,1,0:T(1,128)} %scal_ref.1, bf16[1,1,2048,2048]{3,2,1,0:T(8,128)(2,1)} %inv_hbm.1, bf16[1,1,24,2048]{3,2,1,0:T(8,128)(2,1)} %basis_ref.1, s32[1,1,24]{2,1,0:T(1,128)} %pmap_ref.1, s32[1,1,10,256]{3,2,1,0:T(8,128)} %copy.10.sidx_ref, ...), custom_call_target="tpu_custom_call" | custom-call | tf_op jit(solution)/shard_map/pallas_call | solution.py:492
  84.1 3.0 %copy.12 = f32[1,1,2048,256]{3,2,1,0:T(8,128)} copy(f32[1,1,2048,256]{3,2,1,0:T(8,128)} %shard_map.91) | data formatting | bytes 4194304

commit v2 on v1

--- a/solution.py
+++ b/solution.py
@@ -18,8 +18,12 @@
 G = 192
 CH = R // NN
 PIECE = G // NN
+PIVOT_PIECE = 32
 CARRY = CH + G
 TILE = 256
+HALF = 512
+PACK = TILE // 8
+EARLY = 4
 
 
 def owner_z(n):
@@ -60,13 +64,14 @@
     res_hbm, scal_ref, inv_hbm, basis_ref, pmap_ref, sidx_ref, slen_ref, sub_hbm, piv_hbm,
     out_hbm,
     res, inv, wgt, local, rows, ext, select, pick_out, pick_in, inc, result,
+    part_in, ext_in, weight_in, own_ext, pivot_rows, pivot_out,
     idxm, tiles, maps, spread_map, vals, xfull, stack,
     prim_in, prim_v, sub, piv, chain, rhs, planes, high_carry, pivoted, xs, xplanes, carry,
-    load_sem, inv_sem, out_sem,
+    load_sem, pivot_sem, inv_sem, out_sem,
     prim_send, prim_recv, sub_send, sub_recv, piv_send, piv_recv,
     map_send, map_recv, pick_send, pick_recv,
     y_send, y_recv, t_send, t_recv, b_send, b_recv,
-    x_send, x_recv, gather_send, gather_recv, val_send, val_recv,
+    x_send, x_recv, gather_send, gather_recv, val_send, val_recv, go_sem,
 ):
     w = lax.axis_index("wide")
     n = lax.axis_index("narrow")
@@ -76,15 +81,19 @@
     above = lax.rem(w + 1, NY * NZ)
     below = lax.rem(w + NY * NZ - 1, NY * NZ)
     is_owner = z == owner_z(n)
+    inner = jnp.logical_and(y > 0, y < NY - 1)
 
     load = pltpu.make_async_copy(res_hbm.at[0, 0], res, load_sem)
     load.start()
+    pivot_at = pl.ds(pl.multiple_of(PIVOT_PIECE * jnp.minimum(n, 5), PIVOT_PIECE), PIVOT_PIECE)
+    pivot_load = pltpu.make_async_copy(piv_hbm.at[0, pivot_at], pivot_rows, pivot_sem)
+    pivot_load.start()
 
     def inv_load(i):
-        at = pl.ds(pl.multiple_of(i * TILE, TILE), TILE)
+        at = pl.ds(pl.multiple_of(i * HALF, HALF), HALF)
         return pltpu.make_async_copy(inv_hbm.at[0, 0, at], inv.at[at], inv_sem.at[i])
 
-    @pl.loop(0, NI // TILE)
+    @pl.loop(0, NI // HALF)
     def _(i):
         inv_load(i).start()
 
@@ -100,10 +109,12 @@
 
     @pl.when(is_owner)
     def _():
-        @pl.loop(1, NZ * NN)
-        def _(d):
-            at = lax.rem(z * NN + n + d, NZ * NN)
-            hello((base + at // NN, at % NN))
+        @pl.loop(0, NZ)
+        def _(v):
+            for c in range(NN):
+                @pl.when(jnp.logical_or(v != z, c != n))
+                def _(c=c):
+                    hello((base + v, c))
 
         for d in range(1, NY):
             hello((lax.rem(y + d, NY) * NZ + z, n))
@@ -118,12 +129,12 @@
     for c in range(3):
         stack[32 * c : 32 * c + PC] = basis.astype(f32)
     for c, term in enumerate(split3(scal)):
-        stack[96 + c : 97 + c] = term.astype(f32)
-    stack[99:100] = scal
+        stack[PC + c : PC + c + 1] = term.astype(f32)
+    stack[27:28] = scal
     for i in range(NI // 128):
         ext[128 * i : 128 * i + 128] = stack[:, 128 * i : 128 * i + 128].T
     load.wait()
-    wgt[...] = (ext[:, 99:100] * res[...].astype(f32)).astype(bf16)
+    wgt[...] = (ext[:, 27:28] * res[...].astype(f32)).astype(bf16)
     primal = nn(basis, wgt[...])
 
     pm = jnp.broadcast_to(pmap_ref[0].astype(f32), (PC, PC))
@@ -148,6 +159,9 @@
     def owned(c):
         return jnp.logical_and(is_owner, c == n)
 
+    def turn(i):
+        return lax.rem(i + n + z, NN)
+
     def deliver(src, dst, send, recv, device, here):
         @pl.when(here)
         def _():
@@ -175,7 +189,7 @@
         return (sub_hbm.at[0, piece_at], sub.at[z, piece_at], sub_send.at[c], sub_recv.at[z], (base + owner_z(c), c), owned(c))
 
     def piv_args(c):
-        return (piv_hbm.at[0, piece_at], piv.at[z, piece_at], piv_send.at[c], piv_recv, (base + owner_z(c), c), owned(c))
+        return (pivot_out, piv.at[z, pivot_at], piv_send.at[c], piv_recv, (base + owner_z(c), c), owned(c))
 
     def map_copy(c):
         return pltpu.make_async_remote_copy(
@@ -186,14 +200,17 @@
     def in_map(c):
         return pltpu.make_async_copy(maps.at[c], maps.at[c], map_recv.at[c])
 
-    for args in (prim_args, sub_args):
-        @pl.loop(0, NN)
-        def _(c, args=args):
-            deliver(*args(c))
-
     @pl.loop(0, NN)
-    def _(c):
-        deliver(*piv_args(c))
+    def _(i):
+        deliver(*prim_args(turn(i)))
+
+    @pl.loop(0, NN)
+    def _(i):
+        deliver(*sub_args(turn(i)))
+
+    @pl.loop(0, NN)
+    def _(i):
+        c = turn(i)
 
         @pl.when(c != n)
         def _():
@@ -201,21 +218,36 @@
 
     maps[n] = tiles[0]
 
-    rows[:, 512:640] = ext[...].astype(bf16)
-
-    @pl.loop(0, NI // TILE)
-    def _(i):
-        at = pl.ds(pl.multiple_of(i * TILE, TILE), TILE)
+    own_ext[...] = ext[...].astype(bf16)
+    rows[:, 256:384] = jnp.where(iota((NI, 128), 1) < 32, ext[...], 0.0).astype(bf16)
+
+    @pl.loop(0, NI // HALF)
+    def _(i):
+        at = pl.ds(pl.multiple_of(i * HALF, HALF), HALF)
         inv_load(i).wait()
         part = nn(inv[at], wgt[...])
         local[at] = part
-        high, low = split2(part)
-        rows[at, 0:256] = high
-        rows[at, 256:512] = low
+        rows[at, 0:256] = part.astype(bf16)
 
     slot_lane = iota((1, TILE), 1)
     for k in range(NS):
-        idxm[k : k + 1] = jnp.where(slot_lane < slen_ref[0, 0, k], sidx_ref[0, 0, k : k + 1], -1)
+        idxm[k : k + 1] = jnp.where(slot_lane < slen_ref[0, 0, k], sidx_ref[0, k], -1)
+
+    @pl.loop(0, NI // TILE)
+    def _(i):
+        at = pl.ds(pl.multiple_of(i * TILE, TILE), TILE)
+        row_id = iota((TILE, TILE), 0) + i * TILE
+        for k in range(NS):
+            select[at, TILE * k : TILE * k + TILE] = jnp.where(idxm[k : k + 1] == row_id, 1.0, 0.0).astype(bf16)
+
+    pivot_load.wait()
+    pivot_out[...] = pivot_rows[...].astype(bf16)
+
+    @pl.when(n < G // PIVOT_PIECE)
+    def _():
+        @pl.loop(0, NN)
+        def _(i):
+            deliver(*piv_args(turn(i)))
 
     def pick_copy(k):
         to_w = jnp.where(k == 8, below, jnp.where(k == 9, above, w))
@@ -229,15 +261,34 @@
     def in_pick(k):
         return pltpu.make_async_copy(pick_in.at[k], pick_in.at[k], pick_recv.at[k])
 
-    @pl.loop(0, NS)
-    def _(k):
-        @pl.when(k != n)
-        def _():
-            row = jnp.broadcast_to(idxm[pl.ds(k, 1)].astype(f32), (TILE, TILE))
-            col = jnp.sum(jnp.where(iota((TILE, TILE), 0) == iota((TILE, TILE), 1), row, 0.0), axis=1, keepdims=True)
-            hot = jnp.where(col.astype(jnp.int32) == iota((TILE, NI), 1), 1.0, 0.0).astype(bf16)
-            pick_out[k] = nn(hot, rows[...]).astype(bf16)
-            pick_copy(k).start()
+    def slot_at(i):
+        return jnp.where(i < NN - 1, lax.rem(n + i + 1, NN), i + 1)
+
+    def pick(i):
+        k = slot_at(i)
+        row = jnp.broadcast_to(idxm[pl.ds(k, 1)].astype(f32), (TILE, TILE))
+        col = jnp.sum(jnp.where(iota((TILE, TILE), 0) == iota((TILE, TILE), 1), row, 0.0), axis=1, keepdims=True)
+        hot = jnp.where(col.astype(jnp.int32) == iota((TILE, NI), 1), 1.0, 0.0).astype(bf16)
+        picked = nn(hot, rows[...])
+        pick_out[k, 0:TILE] = picked[:, 0:256].astype(bf16)
+        for g in range(2):
+            packed = picked[PACK * 4 * g : PACK * 4 * g + PACK, 256:384]
+            for q in range(1, 4):
+                at = PACK * (4 * g + q)
+                packed = packed + pltpu.roll(picked[at : at + PACK, 256:384], 32 * q, 1)
+            pick_out[k, TILE : TILE + PACK, 128 * g : 128 * g + 128] = packed.astype(bf16)
+
+    pl.loop(0, jnp.where(is_owner, EARLY, NS - 1))(pick)
+
+    def send_picks(first, last):
+        @pl.loop(first, last)
+        def _(i):
+            pick_copy(slot_at(i)).start()
+
+    @pl.when(jnp.logical_not(is_owner))
+    def _():
+        pl.semaphore_wait(go_sem, 1)
+        send_picks(0, NS - 1)
 
     def y_copies(d):
         device = (lax.rem(y + d, NY) * NZ + z, n)
@@ -281,25 +332,44 @@
         def in_sub(v):
             pltpu.make_async_copy(sub.at[v], sub.at[v], sub_recv.at[v]).wait()
 
+        for v in range(NZ):
+            in_sub(v)
+
+        @pl.loop(0, NZ)
+        def _(v):
+            @pl.when(v != z)
+            def _():
+                pl.semaphore_signal(go_sem, inc=1, device_id=(base + v, n), device_id_type=MESH)
+
         eye = jnp.where(iota((G, G), 0) == iota((G, G), 1), 1.0, 0.0)
-        in_sub(0)
         chain[0, 0:CH] = rhs[0]
         first_high, first_low = split2(sub[0])
         chain[0, CH:CARRY] = -(nt(eye.astype(bf16), first_high) + nt(eye.astype(bf16), first_low))
 
         @pl.loop(1, NZ)
         def _(v):
-            in_sub(v)
             step = dot3(nt, chain[v - 1], sub[v])
             chain[v, 0:CH] = rhs[v] - step[0:CH]
             chain[v, CH:CARRY] = -step[CH:CARRY]
 
         for d in range(1, NY):
             y_copies(d)[0].start()
-        for d in range(1, NY):
-            y_copies(d)[1].start()
+
+        @pl.when(inner)
+        def _():
+            for d in range(1, NY):
+                y_copies(d)[1].start()
+
         planes[y] = chain[NZ - 1]
-        high_carry[NZ - 1] = -eye
+
+        send_picks(0, EARLY)
+
+    pl.loop(jnp.where(is_owner, EARLY, NS - 1), NS - 1)(pick)
+
+    @pl.when(is_owner)
+    def _():
+        send_picks(EARLY, NS - 1)
+        high_carry[NZ - 1] = -jnp.where(iota((G, G), 0) == iota((G, G), 1), 1.0, 0.0)
 
         @pl.loop(0, NZ - 1)
         def _(i):
@@ -308,33 +378,18 @@
 
         pltpu.make_async_copy(piv, piv, piv_recv).wait()
 
-    @pl.loop(0, NI // TILE)
-    def _(i):
-        at = pl.ds(pl.multiple_of(i * TILE, TILE), TILE)
-        row_id = iota((TILE, TILE), 0) + i * TILE
-        for k in range(NS):
-            select[at, TILE * k : TILE * k + TILE] = jnp.where(idxm[k : k + 1] == row_id, 1.0, 0.0).astype(bf16)
-
-    @pl.loop(0, NN)
-    def _(c):
-        @pl.when(c != n)
-        def _():
-            in_map(c).wait()
-
-    for c in range(NN):
-        tile = maps[c]
-        for a in range(3):
-            col = tile[:, 96 + a : 97 + a].astype(jnp.int32)
-            spread_map[32 * c + 8 * a : 32 * c + 8 * a + 8] = jnp.where(col == iota((8, G), 1), 1.0, 0.0)
-        spread_map[32 * c + PC : 32 * c + 32] = jnp.zeros((32 - PC, G), f32)
-    vals[:, 96:128] = jnp.zeros((NS, 32, R), bf16)
-
     @pl.when(is_owner)
     def _():
         def in_plane(d):
             src = lax.rem(y + NY - d, NY)
-            for part, recv in ((pl.ds(0, CH), y_recv), (pl.ds(CH, G), t_recv)):
-                pltpu.make_async_copy(planes.at[src, part], planes.at[src, part], recv.at[src]).wait()
+            values = planes.at[src, pl.ds(0, CH)]
+            pltpu.make_async_copy(values, values, y_recv.at[src]).wait()
+
+            @pl.when(jnp.logical_and(src > 0, src < NY - 1))
+            def _():
+                product = planes.at[src, pl.ds(CH, G)]
+                pltpu.make_async_copy(product, product, t_recv.at[src]).wait()
+
 
         for d in range(1, NY):
             in_plane(d)
@@ -346,7 +401,8 @@
 
         for v in range(NZ):
             solved = chain[v, 0:CH] + dot3(nn, carry[...], chain[v, CH:CARRY])
-            pivoted[v] = dot3(nn, solved, piv[v])
+            high, low = split2(solved)
+            pivoted[v] = nn(high, piv[v]) + nn(low, piv[v])
         xs[NZ - 1] = pivoted[NZ - 1]
 
         @pl.loop(0, NZ - 1)
@@ -385,6 +441,44 @@
     def _(d):
         gather_copy(lax.rem(n + d, NN)).start()
 
+    @pl.loop(0, NN)
+    def _(c):
+        @pl.when(c != n)
+        def _():
+            in_map(c).wait()
+
+    for c in range(NN):
+        tile = maps[c]
+        for a in range(3):
+            col = tile[:, 96 + a : 97 + a].astype(jnp.int32)
+            spread_map[32 * c + 8 * a : 32 * c + 8 * a + 8] = jnp.where(col == iota((8, G), 1), 1.0, 0.0)
+        spread_map[32 * c + PC : 32 * c + 32] = jnp.zeros((32 - PC, G), f32)
+    vals[:, 96:128] = jnp.zeros((NS, 32, R), bf16)
+
+    @pl.loop(0, NS)
+    def _(k):
+        at = pl.ds(pl.multiple_of(k * TILE, TILE), TILE)
+
+        @pl.when(k == n)
+        def _():
+            part_in[at] = jnp.zeros((TILE, R), f32)
+            ext_in[at] = jnp.zeros((TILE, 128), bf16)
+            weight_in[at] = jnp.zeros((TILE, 128), f32)
+
+        @pl.when(k != n)
+        def _():
+            in_pick(k).wait()
+            pieces = []
+            packed = pick_in[k, TILE : TILE + PACK].astype(f32)
+            for q in range(8):
+                piece = packed[:, 128 * (q // 4) : 128 * (q // 4) + 128]
+                pieces.append(pltpu.roll(piece, 128 - 32 * (q % 4), 1) if q % 4 else piece)
+            extra = jnp.where(iota((TILE, 128), 1) < 32, jnp.concatenate(pieces, axis=0), 0.0)
+            weight = extra[:, PC : PC + 1] + extra[:, PC + 1 : PC + 2] + extra[:, PC + 2 : PC + 3]
+            ext_in[at] = (extra + (pltpu.roll(extra, 32, 1) + pltpu.roll(extra, 64, 1))).astype(bf16)
+            weight_in[at] = jnp.broadcast_to(weight, (TILE, 128))
+            part_in[at] = weight * pick_in[k, 0:TILE].astype(f32)
+
     @pl.loop(1, NN)
     def _(d):
         src = lax.rem(n + d, NN)
@@ -408,29 +502,21 @@
         val_copy(side).start()
 
     def receive(k):
-        in_pick(k).wait()
-        picked = pick_in[k]
-        spread = nn(picked[:, 512:640], vals[k])
-        weight = jnp.sum(picked[:, 608:611].astype(f32), axis=1, keepdims=True)
-        part = picked[:, 0:256].astype(f32) + picked[:, 256:512].astype(f32)
-        at = pl.ds(pl.multiple_of(k * TILE, TILE), TILE)
-        inc[at] = (weight * (part + spread)).astype(bf16)
-
-    @pl.loop(0, NN)
-    def _(k):
-        @pl.when(k != n)
-        def _():
-            receive(k)
-
-    own_at = pl.ds(pl.multiple_of(n * TILE, TILE), TILE)
-    inc[own_at] = jnp.zeros((TILE, R), bf16)
-
-    @pl.loop(0, NI // TILE)
-    def _(i):
-        at = pl.ds(pl.multiple_of(i * TILE, TILE), TILE)
-        spread = nn(rows[at, 512:640], vals[n])
-        combined = (ext[at, 99:100] * (local[at] + spread)).astype(bf16)
-        result[at] = combined.astype(f32)
+        at = slice(k * TILE, k * TILE + TILE)
+        spread = nn(ext_in[at], vals[k])
+        weight = weight_in[at]
+        for half in (slice(0, 128), slice(128, 256)):
+            inc[at, half] = (part_in[at, half] + weight * spread[:, half]).astype(bf16)
+
+    for k in range(NN):
+        receive(k)
+
+    @pl.loop(0, NI // HALF)
+    def _(i):
+        at = pl.ds(pl.multiple_of(i * HALF, HALF), HALF)
+        spread = nn(own_ext[at], vals[n])
+        combined = (ext[at, 27:28] * (local[at] + spread)).astype(bf16)
+        result[at] = combined.astype(f32) + nn(select[at, 0 : NN * TILE], inc[0 : NN * TILE])
 
     for side in range(2):
         into = vals.at[8 + side, pl.ds(0, 96)]
@@ -438,20 +524,23 @@
         receive(8 + side)
 
     def store(i):
-        at = pl.ds(pl.multiple_of(i * TILE, TILE), TILE)
+        at = pl.ds(pl.multiple_of(i * HALF, HALF), HALF)
         return pltpu.make_async_copy(result.at[at], out_hbm.at[0, 0, at], out_sem.at[i])
 
-    @pl.loop(0, NI // TILE)
-    def _(i):
-        at = pl.ds(pl.multiple_of(i * TILE, TILE), TILE)
-        result[at] += nn(select[at], inc[...])
+    @pl.loop(0, NI // HALF)
+    def _(i):
+        at = pl.ds(pl.multiple_of(i * HALF, HALF), HALF)
+        result[at] += nn(select[at, NN * TILE : NS * TILE], inc[NN * TILE : NS * TILE])
         store(i).start()
 
     @pl.loop(0, NN)
     def _(c):
         sent(*prim_args(c))
         sent(*sub_args(c))
-        sent(*piv_args(c))
+
+        @pl.when(n < G // PIVOT_PIECE)
+        def _():
+            sent(*piv_args(c))
 
         @pl.when(c != n)
         def _():
@@ -470,15 +559,19 @@
     @pl.when(is_owner)
     def _():
         for d in range(1, NY):
-            for copy in y_copies(d):
-                copy.wait_send()
+            y_copies(d)[0].wait_send()
             back_copy(d).wait_send()
+
+        @pl.when(inner)
+        def _():
+            for d in range(1, NY):
+                y_copies(d)[1].wait_send()
 
         @pl.loop(0, NZ)
         def _(v):
             sent(*x_args(v))
 
-    @pl.loop(0, NI // TILE)
+    @pl.loop(0, NI // HALF)
     def _(i):
         store(i).wait()
 
@@ -495,21 +588,23 @@
         in_specs=[hbm, vmem, hbm, vmem, vmem, vmem, smem, hbm, hbm],
         out_specs=hbm,
         scratch_shapes=[
-            V((NI, R), bf16), V((NI, NI), bf16), V((NI, R), bf16), V((NI, R), f32), V((NI, 640), bf16), V((NI, 128), f32),
-            V((NI, NS * TILE), bf16), V((NS, TILE, 640), bf16), V((NS, TILE, 640), bf16), V((NS * TILE, R), bf16), V((NI, R), f32),
+            V((NI, R), bf16), V((NI, NI), bf16), V((NI, R), bf16), V((NI, R), f32), V((NI, 384), bf16), V((NI, 128), f32),
+            V((NI, NS * TILE), bf16), V((NS, TILE + PACK, 256), bf16), V((NS, TILE + PACK, 256), bf16), V((NS * TILE, R), bf16),
+            V((NI, R), f32), V((NS * TILE, R), f32), V((NS * TILE, 128), bf16), V((NS * TILE, 128), f32), V((NI, 128), bf16),
+            V((PIVOT_PIECE, G), f32), V((PIVOT_PIECE, G), bf16),
             V((16, TILE), jnp.int32), V((NN, 8, 128), f32), V((NN, 8, 128), f32), V((NN * 32, G), f32), V((NS, 128, R), bf16),
             V((R, G), f32), V((128, NI), f32),
-            V((NZ * NN, 8, 128), f32), V((G, 128), f32), V((NZ, G, G), f32), V((NZ, G, G), f32), V((NZ, CARRY, G), f32),
+            V((NZ * NN, 8, 128), f32), V((G, 128), f32), V((NZ, G, G), f32), V((NZ, G, G), bf16), V((NZ, CARRY, G), f32),
             V((NZ, CH, G), f32), V((NY, CARRY, G), f32), V((NZ, G, G), f32), V((NZ, CH, G), f32), V((NZ, CH, G), f32),
             V((NY, CH, G), f32), V((CH, G), f32),
-            dma, dma((NI // TILE,)), dma((NI // TILE,)),
+            dma, dma, dma((NI // HALF,)), dma((NI // HALF,)),
             dma((NN,)), dma, dma((NN,)), dma((NZ,)), dma((NN,)), dma,
             dma((NN,)), dma((NN,)), dma((NS,)), dma((NS,)),
             dma((NY - 1,)), dma((NY,)), dma((NY - 1,)), dma((NY,)), dma((NY - 1,)), dma((NY,)),
-            dma((NZ,)), dma, dma((NN,)), dma((NN,)), dma((2,)), dma((2,)),
+            dma((NZ,)), dma, dma((NN,)), dma((NN,)), dma((2,)), dma((2,)), pltpu.SemaphoreType.REGULAR,
         ],
         compiler_params=pltpu.CompilerParams(collective_id=0, has_side_effects=True, vmem_limit_bytes=58 * 2**20),
-    )(residual, scaling, inverse, basis, primal_map, slot_index, slot_length, sub, pivot)
+    )(residual, scaling, inverse, basis, primal_map, slot_index.transpose(0, 2, 1, 3), slot_length, sub, pivot)
 
 
 def solution(mesh):

time: 87.3 us -> 74.5 us (0.85)
  Pallas kernels: 82.7 us -> 71.3 us
  local copies, waits for them, and re-layouts: 4.35 us -> 3.05 us
    pallas_call x1, Pallas kernels: 82.7 us -> 71.3 us  [body(): pl.pallas_call(kernel, out_shape=jax.ShapeDtypeStruct((1, 1, NI, R), f32)...]
    unnamed x2 -> x1, local copies, waits for them, and re-layouts: 4.35 us -> 3.05 us
where the time goes in v2:
time: 74.5 us; the launch traced here: 74.3 us
  Pallas kernels  71.3 us (96%)
  local copies, waits for them, and re-layouts  3.05 us (4%)
    pallas_call x1, Pallas kernels, body(): pl.pallas_call(kernel, out_shape=jax.ShapeDtypeStruct((1, 1, NI, R), f32)...  71.3 us
    unnamed x1, local copies, waits for them, and re-layouts  3.05 us

profile of v2, /device:TPU:1, one launch (start us, length us, event | category | flops | bytes accessed | tf_op | source)
XLA Modules:
  0.0 74.3 jit_solution(5807697909660851928)
XLA Ops:
  0.0 71.3 %shard_map.91 = f32[1,1,2048,256]{3,2,1,0:T(8,128)} custom-call(bf16[1,1,2048,256]{3,2,1,0:T(8,128)(2,1)} %res_hbm.1, f32[1,1,2048]{2,1,0:T(1,128)} %scal_ref.1, bf16[1,1,2048,2048]{3,2,1,0:T(8,128)(2,1)} %inv_hbm.1, bf16[1,1,24,2048]{3,2,1,0:T(8,128)(2,1)} %basis_ref.1, s32[1,1,24]{2,1,0:T(1,128)} %pmap_ref.1, s32[1,10,1,256]{3,2,1,0:T(1,128)} %bitcast.1, ...), custom_call_target="tpu_custom_call" | custom-call | tf_op jit(solution)/shard_map/pallas_call | solution.py:585
  71.3 3.0 %copy.11 = f32[1,1,2048,256]{3,2,1,0:T(8,128)} copy(f32[1,1,2048,256]{3,2,1,0:T(8,128)} %shard_map.91) | data formatting | bytes 4194304

commit v3 on v2

--- a/solution.py
+++ b/solution.py
@@ -66,7 +66,7 @@
     res, inv, wgt, local, rows, ext, select, pick_out, pick_in, inc, result,
     part_in, ext_in, weight_in, own_ext, pivot_rows, pivot_out,
     idxm, tiles, maps, spread_map, vals, xfull, stack,
-    prim_in, prim_v, sub, piv, chain, rhs, planes, high_carry, pivoted, xs, xplanes, carry,
+    prim_in, prim_v, sub, piv, chain, rhs, planes, high_carry, pivoted, xs, xplanes, carry, x_out, product_out, products,
     load_sem, pivot_sem, inv_sem, out_sem,
     prim_send, prim_recv, sub_send, sub_recv, piv_send, piv_recv,
     map_send, map_recv, pick_send, pick_recv,
@@ -83,6 +83,33 @@
     is_owner = z == owner_z(n)
     inner = jnp.logical_and(y > 0, y < NY - 1)
 
+    barrier = pltpu.get_barrier_semaphore()
+
+    def hello(device):
+        pl.semaphore_signal(barrier, inc=1, device_id=device, device_id_type=MESH)
+
+    @pl.when(is_owner)
+    def _():
+        @pl.loop(0, NZ)
+        def _(i):
+            v = lax.rem(z + NZ // 2 + i, NZ)
+            for c in range(NN):
+                @pl.when(jnp.logical_or(v != z, c != n))
+                def _(c=c):
+                    hello((base + v, c))
+
+        for d in range(1, NY):
+            hello((lax.rem(y + d, NY) * NZ + z, n))
+
+    @pl.when(jnp.logical_not(is_owner))
+    def _():
+        hello((base + owner_z(n), n))
+
+    for d in range(1, NN):
+        hello((w, lax.rem(n + d, NN)))
+    hello((above, n))
+    hello((below, n))
+
     load = pltpu.make_async_copy(res_hbm.at[0, 0], res, load_sem)
     load.start()
     pivot_at = pl.ds(pl.multiple_of(PIVOT_PIECE * jnp.minimum(n, 5), PIVOT_PIECE), PIVOT_PIECE)
@@ -96,32 +123,6 @@
     @pl.loop(0, NI // HALF)
     def _(i):
         inv_load(i).start()
-
-    barrier = pltpu.get_barrier_semaphore()
-
-    def hello(device):
-        pl.semaphore_signal(barrier, inc=1, device_id=device, device_id_type=MESH)
-
-    for d in range(1, NN):
-        hello((w, lax.rem(n + d, NN)))
-    hello((above, n))
-    hello((below, n))
-
-    @pl.when(is_owner)
-    def _():
-        @pl.loop(0, NZ)
-        def _(v):
-            for c in range(NN):
-                @pl.when(jnp.logical_or(v != z, c != n))
-                def _(c=c):
-                    hello((base + v, c))
-
-        for d in range(1, NY):
-            hello((lax.rem(y + d, NY) * NZ + z, n))
-
-    @pl.when(jnp.logical_not(is_owner))
-    def _():
-        hello((base + owner_z(n), n))
 
     basis = basis_ref[0, 0]
     scal = scal_ref[0]
@@ -292,12 +293,15 @@
 
     def y_copies(d):
         device = (lax.rem(y + d, NY) * NZ + z, n)
+        parts = (
+            (chain.at[NZ - 1, pl.ds(0, CH)], planes.at[y], y_send, y_recv),
+            (product_out, products.at[y], t_send, t_recv),
+        )
         return [
             pltpu.make_async_remote_copy(
-                src_ref=chain.at[NZ - 1, part], dst_ref=planes.at[y, part], send_sem=send.at[d - 1], recv_sem=recv.at[y],
-                device_id=device, device_id_type=MESH,
+                src_ref=src, dst_ref=dst, send_sem=send.at[d - 1], recv_sem=recv.at[y], device_id=device, device_id_type=MESH
             )
-            for part, send, recv in ((pl.ds(0, CH), y_send, y_recv), (pl.ds(CH, G), t_send, t_recv))
+            for src, dst, send, recv in parts
         ]
 
     def back_copy(d):
@@ -309,7 +313,7 @@
     chunk_at = pl.ds(pl.multiple_of(n * CH, CH), CH)
 
     def x_args(v):
-        return (xs.at[v], xfull.at[chunk_at], x_send.at[v], x_recv, (base + v, n), v == z)
+        return (x_out.at[v], xfull.at[chunk_at], x_send.at[v], x_recv, (base + v, n), v == z)
 
     @pl.when(is_owner)
     def _():
@@ -352,6 +356,7 @@
             chain[v, 0:CH] = rhs[v] - step[0:CH]
             chain[v, CH:CARRY] = -step[CH:CARRY]
 
+        product_out[...] = chain[NZ - 1, CH:CARRY].astype(bf16)
         for d in range(1, NY):
             y_copies(d)[0].start()
 
@@ -360,7 +365,7 @@
             for d in range(1, NY):
                 y_copies(d)[1].start()
 
-        planes[y] = chain[NZ - 1]
+        planes[y] = chain[NZ - 1, 0:CH]
 
         send_picks(0, EARLY)
 
@@ -382,22 +387,23 @@
     def _():
         def in_plane(d):
             src = lax.rem(y + NY - d, NY)
-            values = planes.at[src, pl.ds(0, CH)]
+            values = planes.at[src]
             pltpu.make_async_copy(values, values, y_recv.at[src]).wait()
 
             @pl.when(jnp.logical_and(src > 0, src < NY - 1))
             def _():
-                product = planes.at[src, pl.ds(CH, G)]
+                product = products.at[src]
                 pltpu.make_async_copy(product, product, t_recv.at[src]).wait()
 
 
         for d in range(1, NY):
             in_plane(d)
-        carry[...] = jnp.where(y > 0, planes[0, 0:CH], 0.0)
+        carry[...] = jnp.where(y > 0, planes[0], 0.0)
         for g in range(1, NY - 1):
             @pl.when(y > g)
             def _(g=g):
-                carry[...] = planes[g, 0:CH] + dot3(nn, carry[...], planes[g, CH:CARRY])
+                high, low = split2(carry[...])
+                carry[...] = planes[g] + (nn(high, products[g]) + nn(low, products[g]))
 
         for v in range(NZ):
             solved = chain[v, 0:CH] + dot3(nn, carry[...], chain[v, CH:CARRY])
@@ -420,10 +426,11 @@
         for g in range(NY - 2, 0, -1):
             @pl.when(y < g)
             def _(g=g):
-                carry[...] = xplanes[g] + dot3(nt, carry[...], planes[g, CH:CARRY])
+                high, low = split2(carry[...])
+                carry[...] = xplanes[g] + (nt(high, products[g]) + nt(low, products[g]))
 
         for v in range(NZ):
-            xs[v] = xs[v] + dot3(nn, carry[...], high_carry[v])
+            x_out[v] = (xs[v] + dot3(nn, carry[...], high_carry[v])).astype(bf16)
 
         @pl.loop(0, NZ)
         def _(v):
@@ -453,7 +460,7 @@
             col = tile[:, 96 + a : 97 + a].astype(jnp.int32)
             spread_map[32 * c + 8 * a : 32 * c + 8 * a + 8] = jnp.where(col == iota((8, G), 1), 1.0, 0.0)
         spread_map[32 * c + PC : 32 * c + 32] = jnp.zeros((32 - PC, G), f32)
-    vals[:, 96:128] = jnp.zeros((NS, 32, R), bf16)
+    vals[:, 32:128] = jnp.zeros((NS, 96, R), bf16)
 
     @pl.loop(0, NS)
     def _(k):
@@ -486,14 +493,13 @@
         pltpu.make_async_copy(xfull.at[at], xfull.at[at], gather_recv.at[src]).wait()
 
     hot = spread_map[...].astype(bf16)
-    for c, term in enumerate(split3(xfull[...])):
-        picked = nt(hot, term).astype(bf16)
-        for j in range(NN):
-            vals[j, 32 * c : 32 * c + 32] = picked[32 * j : 32 * j + 32]
+    coarse_vals = nt(hot, xfull[...]).astype(bf16)
+    for j in range(NN):
+        vals[j, 0:32] = coarse_vals[32 * j : 32 * j + 32]
 
     def val_copy(side):
         return pltpu.make_async_remote_copy(
-            src_ref=vals.at[n, pl.ds(0, 96)], dst_ref=vals.at[8 + side, pl.ds(0, 96)],
+            src_ref=vals.at[n, pl.ds(0, 32)], dst_ref=vals.at[8 + side, pl.ds(0, 32)],
             send_sem=val_send.at[side], recv_sem=val_recv.at[side],
             device_id=(above if side == 0 else below, n), device_id_type=MESH,
         )
@@ -519,7 +525,7 @@
         result[at] = combined.astype(f32) + nn(select[at, 0 : NN * TILE], inc[0 : NN * TILE])
 
     for side in range(2):
-        into = vals.at[8 + side, pl.ds(0, 96)]
+        into = vals.at[8 + side, pl.ds(0, 32)]
         pltpu.make_async_copy(into, into, val_recv.at[side]).wait()
         receive(8 + side)
 
@@ -593,10 +599,10 @@
             V((NI, R), f32), V((NS * TILE, R), f32), V((NS * TILE, 128), bf16), V((NS * TILE, 128), f32), V((NI, 128), bf16),
             V((PIVOT_PIECE, G), f32), V((PIVOT_PIECE, G), bf16),
             V((16, TILE), jnp.int32), V((NN, 8, 128), f32), V((NN, 8, 128), f32), V((NN * 32, G), f32), V((NS, 128, R), bf16),
-            V((R, G), f32), V((128, NI), f32),
+            V((R, G), bf16), V((128, NI), f32),
             V((NZ * NN, 8, 128), f32), V((G, 128), f32), V((NZ, G, G), f32), V((NZ, G, G), bf16), V((NZ, CARRY, G), f32),
-            V((NZ, CH, G), f32), V((NY, CARRY, G), f32), V((NZ, G, G), f32), V((NZ, CH, G), f32), V((NZ, CH, G), f32),
-            V((NY, CH, G), f32), V((CH, G), f32),
+            V((NZ, CH, G), f32), V((NY, CH, G), f32), V((NZ, G, G), f32), V((NZ, CH, G), f32), V((NZ, CH, G), f32),
+            V((NY, CH, G), f32), V((CH, G), f32), V((NZ, CH, G), bf16), V((G, G), bf16), V((NY, G, G), bf16),
             dma, dma, dma((NI // HALF,)), dma((NI // HALF,)),
             dma((NN,)), dma, dma((NN,)), dma((NZ,)), dma((NN,)), dma,
             dma((NN,)), dma((NN,)), dma((NS,)), dma((NS,)),

time: 74.5 us -> 69.2 us (0.929)
  Pallas kernels: 71.3 us -> 66 us
    pallas_call x1, Pallas kernels: 71.3 us -> 66 us  [body(): pl.pallas_call(kernel, out_shape=jax.ShapeDtypeStruct((1, 1, NI, R), f32)...]
where the time goes in v3:
time: 69.2 us; the launch traced here: 69.1 us
  Pallas kernels  66 us (95%)
  local copies, waits for them, and re-layouts  3.05 us (4%)
    pallas_call x1, Pallas kernels, body(): pl.pallas_call(kernel, out_shape=jax.ShapeDtypeStruct((1, 1, NI, R), f32)...  66 us
    unnamed x1, local copies, waits for them, and re-layouts  3.05 us

profile of v3, /device:TPU:1, one launch (start us, length us, event | category | flops | bytes accessed | tf_op | source)
XLA Modules:
  0.0 69.1 jit_solution(8787490245803398607)
XLA Ops:
  0.0 66.0 %shard_map.91 = f32[1,1,2048,256]{3,2,1,0:T(8,128)} custom-call(bf16[1,1,2048,256]{3,2,1,0:T(8,128)(2,1)} %res_hbm.1, f32[1,1,2048]{2,1,0:T(1,128)} %scal_ref.1, bf16[1,1,2048,2048]{3,2,1,0:T(8,128)(2,1)} %inv_hbm.1, bf16[1,1,24,2048]{3,2,1,0:T(8,128)(2,1)} %basis_ref.1, s32[1,1,24]{2,1,0:T(1,128)} %pmap_ref.1, s32[1,10,1,256]{3,2,1,0:T(1,128)} %bitcast.1, ...), custom_call_target="tpu_custom_call" | custom-call | tf_op jit(solution)/shard_map/pallas_call | solution.py:591
  66.1 3.0 %copy.11 = f32[1,1,2048,256]{3,2,1,0:T(8,128)} copy(f32[1,1,2048,256]{3,2,1,0:T(8,128)} %shard_map.91) | data formatting | bytes 4194304

commit v4 on v3

--- a/solution.py
+++ b/solution.py
@@ -66,7 +66,7 @@
     res, inv, wgt, local, rows, ext, select, pick_out, pick_in, inc, result,
     part_in, ext_in, weight_in, own_ext, pivot_rows, pivot_out,
     idxm, tiles, maps, spread_map, vals, xfull, stack,
-    prim_in, prim_v, sub, piv, chain, rhs, planes, high_carry, pivoted, xs, xplanes, carry, x_out, product_out, products,
+    prim_in, prim_v, sub, piv, chain, rhs, planes, high_carry, pivoted, xs, xplanes, carry, product_out, products,
     load_sem, pivot_sem, inv_sem, out_sem,
     prim_send, prim_recv, sub_send, sub_recv, piv_send, piv_recv,
     map_send, map_recv, pick_send, pick_recv,
@@ -313,7 +313,7 @@
     chunk_at = pl.ds(pl.multiple_of(n * CH, CH), CH)
 
     def x_args(v):
-        return (x_out.at[v], xfull.at[chunk_at], x_send.at[v], x_recv, (base + v, n), v == z)
+        return (xs.at[v], xfull.at[chunk_at], x_send.at[v], x_recv, (base + v, n), v == z)
 
     @pl.when(is_owner)
     def _():
@@ -430,7 +430,7 @@
                 carry[...] = xplanes[g] + (nt(high, products[g]) + nt(low, products[g]))
 
         for v in range(NZ):
-            x_out[v] = (xs[v] + dot3(nn, carry[...], high_carry[v])).astype(bf16)
+            xs[v] = xs[v] + dot3(nn, carry[...], high_carry[v])
 
         @pl.loop(0, NZ)
         def _(v):
@@ -460,7 +460,7 @@
             col = tile[:, 96 + a : 97 + a].astype(jnp.int32)
             spread_map[32 * c + 8 * a : 32 * c + 8 * a + 8] = jnp.where(col == iota((8, G), 1), 1.0, 0.0)
         spread_map[32 * c + PC : 32 * c + 32] = jnp.zeros((32 - PC, G), f32)
-    vals[:, 32:128] = jnp.zeros((NS, 96, R), bf16)
+    vals[:, 96:128] = jnp.zeros((NS, 32, R), bf16)
 
     @pl.loop(0, NS)
     def _(k):
@@ -493,13 +493,14 @@
         pltpu.make_async_copy(xfull.at[at], xfull.at[at], gather_recv.at[src]).wait()
 
     hot = spread_map[...].astype(bf16)
-    coarse_vals = nt(hot, xfull[...]).astype(bf16)
-    for j in range(NN):
-        vals[j, 0:32] = coarse_vals[32 * j : 32 * j + 32]
+    for c, term in enumerate(split3(xfull[...])):
+        picked = nt(hot, term).astype(bf16)
+        for j in range(NN):
+            vals[j, 32 * c : 32 * c + 32] = picked[32 * j : 32 * j + 32]
 
     def val_copy(side):
         return pltpu.make_async_remote_copy(
-            src_ref=vals.at[n, pl.ds(0, 32)], dst_ref=vals.at[8 + side, pl.ds(0, 32)],
+            src_ref=vals.at[n, pl.ds(0, 96)], dst_ref=vals.at[8 + side, pl.ds(0, 96)],
             send_sem=val_send.at[side], recv_sem=val_recv.at[side],
             device_id=(above if side == 0 else below, n), device_id_type=MESH,
         )
@@ -525,7 +526,7 @@
         result[at] = combined.astype(f32) + nn(select[at, 0 : NN * TILE], inc[0 : NN * TILE])
 
     for side in range(2):
-        into = vals.at[8 + side, pl.ds(0, 32)]
+        into = vals.at[8 + side, pl.ds(0, 96)]
         pltpu.make_async_copy(into, into, val_recv.at[side]).wait()
         receive(8 + side)
 
@@ -599,10 +600,10 @@
             V((NI, R), f32), V((NS * TILE, R), f32), V((NS * TILE, 128), bf16), V((NS * TILE, 128), f32), V((NI, 128), bf16),
             V((PIVOT_PIECE, G), f32), V((PIVOT_PIECE, G), bf16),
             V((16, TILE), jnp.int32), V((NN, 8, 128), f32), V((NN, 8, 128), f32), V((NN * 32, G), f32), V((NS, 128, R), bf16),
-            V((R, G), bf16), V((128, NI), f32),
+            V((R, G), f32), V((128, NI), f32),
             V((NZ * NN, 8, 128), f32), V((G, 128), f32), V((NZ, G, G), f32), V((NZ, G, G), bf16), V((NZ, CARRY, G), f32),
             V((NZ, CH, G), f32), V((NY, CH, G), f32), V((NZ, G, G), f32), V((NZ, CH, G), f32), V((NZ, CH, G), f32),
-            V((NY, CH, G), f32), V((CH, G), f32), V((NZ, CH, G), bf16), V((G, G), bf16), V((NY, G, G), bf16),
+            V((NY, CH, G), f32), V((CH, G), f32), V((G, G), bf16), V((NY, G, G), bf16),
             dma, dma, dma((NI // HALF,)), dma((NI // HALF,)),
             dma((NN,)), dma, dma((NN,)), dma((NZ,)), dma((NN,)), dma,
             dma((NN,)), dma((NN,)), dma((NS,)), dma((NS,)),

time: 69.2 us -> 70.9 us (1.025)
  Pallas kernels: 66 us -> 67.7 us
    pallas_call x1, Pallas kernels: 66 us -> 67.7 us  [body(): pl.pallas_call(kernel, out_shape=jax.ShapeDtypeStruct((1, 1, NI, R), f32)...]
where the time goes in v4:
time: 70.9 us; the launch traced here: 70.8 us
  Pallas kernels  67.7 us (95%)
  local copies, waits for them, and re-layouts  3.05 us (4%)
    pallas_call x1, Pallas kernels, body(): pl.pallas_call(kernel, out_shape=jax.ShapeDtypeStruct((1, 1, NI, R), f32)...  67.7 us
    unnamed x1, local copies, waits for them, and re-layouts  3.05 us

profile of v4, /device:TPU:1, one launch (start us, length us, event | category | flops | bytes accessed | tf_op | source)
XLA Modules:
  0.0 70.8 jit_solution(1661560240692123589)
XLA Ops:
  0.0 67.7 %shard_map.91 = f32[1,1,2048,256]{3,2,1,0:T(8,128)} custom-call(bf16[1,1,2048,256]{3,2,1,0:T(8,128)(2,1)} %res_hbm.1, f32[1,1,2048]{2,1,0:T(1,128)} %scal_ref.1, bf16[1,1,2048,2048]{3,2,1,0:T(8,128)(2,1)} %inv_hbm.1, bf16[1,1,24,2048]{3,2,1,0:T(8,128)(2,1)} %basis_ref.1, s32[1,1,24]{2,1,0:T(1,128)} %pmap_ref.1, s32[1,10,1,256]{3,2,1,0:T(1,128)} %bitcast.1, ...), custom_call_target="tpu_custom_call" | custom-call | tf_op jit(solution)/shard_map/pallas_call | solution.py:592
  67.8 3.0 %copy.11 = f32[1,1,2048,256]{3,2,1,0:T(8,128)} copy(f32[1,1,2048,256]{3,2,1,0:T(8,128)} %shard_map.91) | data formatting | bytes 4194304

commit v5 on v4

--- a/solution.py
+++ b/solution.py
@@ -23,7 +23,7 @@
 TILE = 256
 HALF = 512
 PACK = TILE // 8
-EARLY = 4
+EARLY = 6
 
 
 def owner_z(n):
@@ -432,9 +432,8 @@
         for v in range(NZ):
             xs[v] = xs[v] + dot3(nn, carry[...], high_carry[v])
 
-        @pl.loop(0, NZ)
-        def _(v):
-            deliver(*x_args(v))
+        for d in (4, 3, 5, 2, 6, 1, 7, 0):
+            deliver(*x_args(lax.rem(z + d, NZ)))
 
     def gather_copy(c):
         return pltpu.make_async_remote_copy(

time: 70.9 us -> 69.3 us (0.977)
  Pallas kernels: 67.7 us -> 66.1 us
    pallas_call x1, Pallas kernels: 67.7 us -> 66.1 us  [body(): pl.pallas_call(kernel, out_shape=jax.ShapeDtypeStruct((1, 1, NI, R), f32)...]
where the time goes in v5:
time: 69.3 us; the launch traced here: 69.1 us
  Pallas kernels  66.1 us (95%)
  local copies, waits for them, and re-layouts  3.05 us (4%)
    pallas_call x1, Pallas kernels, body(): pl.pallas_call(kernel, out_shape=jax.ShapeDtypeStruct((1, 1, NI, R), f32)...  66.1 us
    unnamed x1, local copies, waits for them, and re-layouts  3.05 us

profile of v5, /device:TPU:1, one launch (start us, length us, event | category | flops | bytes accessed | tf_op | source)
XLA Modules:
  0.0 69.1 jit_solution(6026917719414247096)
XLA Ops:
  0.0 66.1 %shard_map.91 = f32[1,1,2048,256]{3,2,1,0:T(8,128)} custom-call(bf16[1,1,2048,256]{3,2,1,0:T(8,128)(2,1)} %res_hbm.1, f32[1,1,2048]{2,1,0:T(1,128)} %scal_ref.1, bf16[1,1,2048,2048]{3,2,1,0:T(8,128)(2,1)} %inv_hbm.1, bf16[1,1,24,2048]{3,2,1,0:T(8,128)(2,1)} %basis_ref.1, s32[1,1,24]{2,1,0:T(1,128)} %pmap_ref.1, s32[1,10,1,256]{3,2,1,0:T(1,128)} %bitcast.1, ...), custom_call_target="tpu_custom_call" | custom-call | tf_op jit(solution)/shard_map/pallas_call | solution.py:591
  66.1 3.0 %copy.11 = f32[1,1,2048,256]{3,2,1,0:T(8,128)} copy(f32[1,1,2048,256]{3,2,1,0:T(8,128)} %shard_map.91) | data formatting | bytes 4194304
